TPU v7x, 512 devices: a whole 4x4x16 slice. The times are simulated.
512 devices in a mesh: ctx: 64 (over z_hi, x, y), tp: 8 (over z_lo, core).
Axes of the slice: x: 4, y: 4, z: 16 (z_hi: 4, z_lo: 4; z = z_hi * 4 + z_lo), core: 2. Of those that a mesh axis runs over, the one named last changes fastest.
Arguments:
- queries: bfloat16 [8192, 32, 128], P('ctx', 'tp'), may hold values from -14 to 14
- keys: bfloat16 [8192, 4, 128], P('ctx'), may hold values from -14 to 14
- values: bfloat16 [8192, 4, 128], P('ctx'), may hold values from -6 to 6
- segment_ids: int32 [8192], P('ctx'), may hold values from 0 to 1, never falling along the last dimension, each value on 1 to 6144 neighbouring positions
- out_weight: bfloat16 [4096, 8192], P('tp', 'ctx'), may hold values from -0.375 to 0.375
Outputs:
- projected: bfloat16 [8192, 8192], P('ctx', 'tp')
Inputs may be any that keep to these rules, and one draw needn't show every extreme that they name: `segment_ids`: document ids never fall along the window; the longest document holds at most 6144 tokens.
All inputs are finite; a program needn't handle non-finite values.
Results may differ from a plain program's by a relative error of at most 0.017.
Values may be sent and summed in bfloat16 or wider, within the bound.
A program may use at most 128 MiB of HBM per device.

v0:
```python
import math

import jax
import jax.numpy as jnp
from jax import lax
from jax.sharding import PartitionSpec as P

HQ = 32
KVH = 4
QB = 128


def hadamard_table(order_size):
    position = jnp.arange(order_size)
    parity = jnp.zeros((order_size, order_size), jnp.int32)
    for level in range(order_size.bit_length() - 1):
        step_bit = 2**level
        parity = parity + position[:, None] // step_bit % 2 * (position[None, :] // step_bit % 2)
    return jnp.where(parity % 2 == 0, 1.0, -1.0).astype(jnp.float32) / math.sqrt(order_size)


def rotate_blocks(partial_value):
    row_count, col_count = partial_value.shape
    rotation = hadamard_table(QB)
    result = jnp.einsum(
        "rbq,qp->rbp",
        partial_value.reshape(row_count, col_count // QB, QB),
        rotation,
        precision=lax.Precision.HIGHEST,
    )
    return result.reshape(row_count, col_count)


def body(queries, keys, values, segment_ids, out_weight):
    row_count, local_heads, head_dim = queries.shape
    group_size = HQ // KVH
    kv_count = max(1, local_heads // group_size)
    per_kv = local_heads // kv_count
    score_scale = head_dim ** (-0.5)
    kv_first = lax.axis_index("tp") * local_heads // group_size
    own_keys = lax.dynamic_slice_in_dim(keys, kv_first, kv_count, 1)
    own_values = lax.dynamic_slice_in_dim(values, kv_first, kv_count, 1)
    grouped = queries.reshape(row_count, kv_count, per_kv, head_dim)
    query_pos = lax.axis_index("ctx") * row_count + jnp.arange(row_count)
    start_top = jnp.full((row_count, kv_count, per_kv), -1e30, jnp.float32)
    top_score = start_top
    part_keys = lax.all_gather(own_keys, "ctx", axis=0, tiled=True)
    part_values = lax.all_gather(own_values, "ctx", axis=0, tiled=True)
    part_segs = lax.all_gather(segment_ids, "ctx", axis=0, tiled=True)
    key_count = part_keys.shape[0]
    scores = (
        jnp.einsum("tngd,knd->tngk", grouped, part_keys, preferred_element_type=jnp.float32)
        * score_scale
    )
    key_pos = jnp.arange(key_count)
    allowed = (segment_ids[:, None] == part_segs[None, :]) & (
        key_pos[None, :] <= query_pos[:, None]
    )
    allowed = allowed[:, None, None, :]
    scores = jnp.where(allowed, scores, -1e30)
    new_top = jnp.maximum(top_score, jnp.max(scores, axis=-1))
    weights = jnp.where(allowed, jnp.exp(scores - new_top[..., None]), 0.0)
    denominator = jnp.sum(weights, axis=-1)
    weighted = jnp.einsum(
        "tngk,knd->tngd", weights, part_values.astype(jnp.float32), precision=lax.Precision.HIGHEST
    )
    top_score, denominator, weighted = (new_top, denominator, weighted)
    attended = (
        (weighted / denominator[..., None])
        .astype(jnp.bfloat16)
        .reshape(row_count, local_heads * head_dim)
    )
    partial_value = jnp.dot(
        attended,
        lax.all_gather(out_weight, "ctx", axis=1, tiled=True),
        preferred_element_type=jnp.float32,
    )
    terms = rotate_blocks(partial_value)
    summed = lax.psum_scatter(terms.astype(jnp.bfloat16), "tp", scatter_dimension=1, tiled=True)
    return summed


def solution(mesh):
    in_specs = (
        P("ctx", "tp", None),
        P("ctx", None, None),
        P("ctx", None, None),
        P("ctx"),
        P("tp", "ctx"),
    )
    out_specs = P("ctx", "tp")
    return jax.shard_map(body, mesh=mesh, in_specs=in_specs, out_specs=out_specs, check_vma=False)
```

profile of v0, /device:TPU:1, one launch (start us, length us, event | category | flops | bytes accessed | tf_op | source)
XLA Modules:
  0.0 567.7 jit_solution(1494587832683764843)
XLA Ops:
  6.5 0.0 copy-start
  6.5 0.0 all-gather.7.cloned.1.call-start
  6.5 1.0 constant_dynamic-slice_fusion
  7.6 0.6 copy.19
  8.2 0.0 all-gather.7.cloned.1.call-update
  8.2 0.0 all-gather.5.cloned.1.call-start
  8.2 1.0 constant_dynamic-slice_fusion.1
  9.2 0.7 copy.18
  9.9 0.0 all-gather.5.cloned.1.call-update
  10.0 0.0 all-gather.9.cloned.1.call-start
  10.0 0.7 all-gather.9.cloned.1.call-update
  10.7 0.0 reduce-scatter.2.cloned.1.call-start
  10.8 202.3 %all-gather = s32[64,1,128]{2,1,0:T(1,128)S(1)} all-gather(s32[1,1,128]{2,1,0:T(1,128)} %bitcast.74), channel_id=1, replica_groups=mesh['ctx'=64,'tp'=8] {'ctx'}, dimensions={0}, use_global_device_ids=true | all-gather | bytes 33280 | tf_op jit(solution)/shard_map/all_gather | solution.py:49
  213.1 4.4 fusion.12
  217.4 0.0 all-gather.7.cloned.1.call-done
  217.5 0.0 copy-done
  217.5 3.8 fusion.2
  221.3 0.0 copy-start.1
  221.3 5.7 %copy-done.1 = f32[8192,128,4]{1,0,2:T(8,128)} copy-done((f32[8192,128,4]{1,0,2:T(8,128)}, f32[8192,128,4]{1,0,2:T(8,128)S(1)}, u32[]{:S(2)}) %copy-start.1) | copy-done | bytes 16777240
  227.0 4.2 fusion.3
  231.2 25.9 %all-gather.5.cloned.1.call-done = bf16[8192,1,128]{0,2,1:T(8,128)(2,1)} async-done(((bf16[128,1,128]{0,2,1:T(8,128)(2,1)}), bf16[8192,1,128]{0,2,1:T(8,128)(2,1)}) %all-gather.5.cloned.1.call-update) | async-done | bytes 2097168 | tf_op jit(solution)/shard_map/all_gather | solution.py:48
  257.1 13.7 %fusion.26 = bf16[1,128,128,4]{2,1,3,0:T(8,128)(2,1)S(1)} fusion(f32[8192,128,4]{1,0,2:T(8,128)} %copy-done.1, f32[128,4]{0,1:T(4,128)S(1)} %broadcast_maximum_fusion, pred[128,8192]{0,1:T(8,128)(4,1)S(1)} %fusion.12, bf16[8192,1,128]{0,2,1:T(8,128)(2,1)} %all-gather.5.cloned.1.call-done, f32[128,4]{0,1:T(4,128)S(1)} %fusion.3), kind=kOutput, calls=%fused_computation.22 | convolution fusion | flops 6459359232 | bytes 20058112 | tf_op jit(solution)/shard_map/tngk,knd->tngd/dot_general | solution.py:64
  270.8 243.8 %all-gather.9.cloned.1.call-done = bf16[512,8192]{1,0:T(8,128)(2,1)} async-done(((bf16[512,128]{1,0:T(8,128)(2,1)}), bf16[512,8192]{1,0:T(8,128)(2,1)}) %all-gather.9.cloned.1.call-update) | async-done | bytes 8388624 | tf_op jit(solution)/shard_map/all_gather | solution.py:75
  514.6 4.8 fusion.4
  519.4 4.2 convolution_convert_fusion
  523.6 2.9 copy.15
  526.5 0.0 reduce-scatter.2.cloned.1.call-update
  526.5 34.6 %reduce-scatter.2.cloned.1.call-done = bf16[128,1024]{1,0:T(8,128)(2,1)} async-done(((bf16[128,8192]{1,0:T(8,128)(2,1)}), bf16[128,1024]{1,0:T(8,128)(2,1)}) %reduce-scatter.2.cloned.1.call-update) | async-done | bytes 262160 | tf_op jit(solution)/shard_map/reduce_scatter | solution.py:79
  (6 shorter events, 0.0 us)
Async XLA Ops:
  6.5 210.9 %copy-start = (bf16[128,4,128]{2,1,0:T(4,128)(2,1)S(1)}, bf16[128,4,128]{2,1,0:T(4,128)(2,1)}, u32[]{:S(2)}) copy-start(bf16[128,4,128]{2,1,0:T(4,128)(2,1)} %param.5) | copy-start | bytes 393220
  6.5 210.9 %all-gather.7.cloned.1.call-start = ((), (), s32[]{:S(2)}) async-start(), calls=%async_computation.2 | async-start | bytes 2129920 | tf_op jit(solution)/shard_map/all_gather | solution.py:47
  8.2 248.9 %all-gather.5.cloned.1.call-start = ((), (), s32[]{:S(2)}) async-start(), calls=%async_computation.1 | async-start | bytes 2129920 | tf_op jit(solution)/shard_map/all_gather | solution.py:48
  10.0 504.7 %all-gather.9.cloned.1.call-start = ((), (), s32[]{:S(2)}) async-start(), calls=%async_computation.3 | async-start | bytes 8519680 | tf_op jit(solution)/shard_map/all_gather | solution.py:75
  10.7 550.4 %reduce-scatter.2.cloned.1.call-start = ((), (), s32[]{:S(2)}) async-start(), calls=%async_computation.4 | async-start | bytes 2359296 | tf_op jit(solution)/shard_map/reduce_scatter | solution.py:79
  221.3 5.7 %copy-start.1 = (f32[8192,128,4]{1,0,2:T(8,128)}, f32[8192,128,4]{1,0,2:T(8,128)S(1)}, u32[]{:S(2)}) copy-start(f32[8192,128,4]{1,0,2:T(8,128)S(1)} %get-tuple-element.6) | copy-start | bytes 50331652
Sparse Core Ops, SparseCore 0:
  11.5 118.3 all-gather.6
  133.9 123.1 all-gather.4
  261.1 253.5 all-gather.8
  526.6 34.4 reduce-scatter.1
where the time goes:
time: 569 us; the launch traced here: 568 us
  waiting for transfers between devices  305 us (54%)
  blocking collectives  202 us (36%)
  matrix products  26.4 us (5%)
  between operations  13.2 us (2%)
  local copies, waits for them, and re-layouts  11.9 us (2%)
  other arithmetic  8.58 us (2%)
    all_gather x1, waiting for transfers between devices, body(): lax.all_gather(out_weight, 'ctx', axis=1, tiled=True)  244 us
    all_gather x1, blocking collectives, body(): part_segs = lax.all_gather(segment_ids, 'ctx', axis=0, tiled=True)  202 us
    reduce_scatter x1, waiting for transfers between devices, body(): lax.psum_scatter(terms.astype(jnp.bfloat16), 'tp', scatter_dimension=1, t...  34.6 us
    all_gather x1, waiting for transfers between devices, body(): part_values = lax.all_gather(own_values, 'ctx', axis=0, tiled=True)  25.9 us
    dot_general x1, matrix products, body(): jnp.einsum('tngk,knd->tngd', weights, part_values.astype(jnp.float32), pr...  13.7 us
  transfers between devices with their start and end apart: 4, of which 3 were waited for; matrix products, arithmetic and copies ran while one was open for 5% of the time, Pallas kernels for 0%

commit v1 on v0

v1 whole, which is shorter than its diff:
```python
import functools
import math

import jax
import jax.numpy as jnp
from jax import lax
from jax.experimental import pallas as pl
from jax.experimental.pallas import tpu as pltpu
from jax.sharding import PartitionSpec as P

HQ = 32
KVH = 4
HD = 128
ROWS = 128
SEG = 16
BLK = ROWS + SEG
NEG = -1e30
MESH = pl.DeviceIdType.MESH
BF16, F32 = jnp.bfloat16, jnp.float32


def mod4(value):
    return lax.rem(value + 8, 4)


def hadamard_signs():
    both = lax.broadcasted_iota(jnp.int32, (HD, HD), 0) & lax.broadcasted_iota(jnp.int32, (HD, HD), 1)
    both = both ^ (both >> 4)
    both = both ^ (both >> 2)
    both = both ^ (both >> 1)
    return (1 - 2 * (both & 1)).astype(F32).astype(BF16)


def kernel(
    q_ref, mine_ref, seg_ref, w_ref, o_ref,
    kv, wb, asrc, ar, pbuf, rb, osrc, ob, segq, top, den, acc,
    kz_s, kz_r, kp_s, kp_r, ks_s, ks_r, wz_s, wz_r, wx_s, wx_r, ws_s, ws_r, a_s, a_r, p_s, p_r, o_s, o_r,
):
    ctx, tpi = lax.axis_index("ctx"), lax.axis_index("tp")
    h, x, y = lax.div(ctx, 16), lax.rem(lax.div(ctx, 4), 4), lax.rem(ctx, 4)
    z, k = lax.div(tpi, 2), lax.rem(tpi, 2)
    xy = x * 4 + y
    other = 1 - k

    def dev(dh=0, dx=0, dy=0, dz=0, core=None):
        return (
            mod4(h + dh) * 16 + mod4(x + dx) * 4 + mod4(y + dy),
            mod4(z + dz) * 2 + (k if core is None else core),
        )

    def copy(src, dst, send, recv, device):
        return pltpu.make_async_remote_copy(
            src_ref=src, dst_ref=dst, send_sem=send, recv_sem=recv, device_id=device, device_id_type=MESH
        )

    sib = dev(core=other)

    barrier = pltpu.get_barrier_semaphore()

    def greet(device):
        pl.semaphore_signal(barrier, inc=1, device_id=device, device_id_type=MESH)

    greet(sib)
    for i in range(1, 4):
        greet(dev(dh=i))
        greet(dev(dz=i))
        greet(dev(dy=i, core=other))

    def greet_plane(d, _):
        greet(dev(dx=lax.div(d, 4), dy=lax.rem(d, 4)))
        return 0

    lax.fori_loop(1, 16, greet_plane, 0)

    kv[k, h, xy, 0:ROWS, :] = mine_ref[...]
    seg_row = seg_ref[...].astype(F32)
    kv[k, h, xy, ROWS:BLK, :] = jnp.broadcast_to(seg_row, (SEG, HD)).astype(BF16)
    rotated = jnp.dot(w_ref[...], hadamard_signs(), preferred_element_type=F32) * (1.0 / math.sqrt(HD))
    wb[k, h, x] = rotated.astype(BF16)
    seg_col = jnp.broadcast_to(seg_row, (ROWS, HD)).T
    for i in range(4):
        segq[i * ROWS : (i + 1) * ROWS, :] = seg_col
    top[...] = jnp.full_like(top, NEG)
    den[...] = jnp.zeros_like(den)
    acc[...] = jnp.zeros_like(acc)

    pl.semaphore_wait(barrier, 25)

    def kv_z(i, out):
        at = kv.at[k, h if out else mod4(h - i), xy]
        return copy(at, at, kz_s.at[i], kz_r.at[i], dev(dh=i))

    def kv_plane(r, d, out):
        dx, dy = lax.div(d, 4), lax.rem(d, 4)
        place = xy if out else mod4(x - dx) * 4 + mod4(y - dy)
        at = kv.at[k, mod4(h - r), place]
        return copy(at, at, kp_s.at[r, d], kp_r.at[r, d], dev(dx=dx, dy=dy))

    def kv_sib(r, dx, out):
        at = kv.at[k if out else other, mod4(h - r), pl.ds(mod4(x - dx) * 4, 4)]
        return copy(at, at, ks_s.at[r, dx], ks_r.at[r, dx], sib)

    def w_z(i, out):
        at = wb.at[k, h if out else mod4(h - i), x]
        return copy(at, at, wz_s.at[i], wz_r.at[i], dev(dh=i))

    def w_x(r, i, out):
        at = wb.at[k, mod4(h - r), x if out else mod4(x - i)]
        return copy(at, at, wx_s.at[r, i], wx_r.at[r, i], dev(dx=i))

    def w_sib(r, out):
        at = wb.at[k if out else other, mod4(h - r)]
        return copy(at, at, ws_s.at[r], ws_r.at[r], sib)

    def a_y(dy, dk, out):
        core = lax.rem(k + dk, 2)
        dst = ar.at[k, y] if out else ar.at[core, mod4(y - dy)]
        return copy(asrc.at[core], dst, a_s.at[dy, dk], a_r.at[dy, dk], dev(dy=dy, core=core))

    def p_z(i, out):
        return copy(pbuf.at[i], rb.at[z if out else mod4(z - i)], p_s.at[i], p_r.at[i], dev(dz=i))

    def o_y(dy, dk, out):
        core = lax.rem(k + dk, 2)
        dst = ob.at[k, y] if out else ob.at[core, mod4(y - dy)]
        return copy(osrc.at[mod4(y + dy), core], dst, o_s.at[dy, dk], o_r.at[dy, dk], dev(dy=dy, core=core))

    pairs = [(dy, dk) for dy in range(4) for dk in range(2) if dy or dk]

    def plane_out(r):
        def step(d, _):
            kv_plane(r, d, True).start()
            return 0

        lax.fori_loop(1, 16, step, 0)

    def plane_in(r):
        def row(dx, _):
            def one(d, _):
                kv_plane(r, d, False).wait_recv()
                return 0

            lax.fori_loop(jnp.maximum(dx * 4, 1), dx * 4 + 4, one, 0)
            kv_sib(r, dx, True).start()
            return 0

        lax.fori_loop(0, 4, row, 0)

    def attend(hp, row, diagonal):
        keys = kv[0, hp, pl.ds(row * 4, 4), 0:ROWS, :].reshape(4 * ROWS, HD)
        values = kv[1, hp, pl.ds(row * 4, 4), 0:ROWS, :].reshape(4 * ROWS, HD)
        ids = kv[0, hp, pl.ds(row * 4, 4), ROWS:BLK, :].astype(F32)
        ids = jnp.concatenate([ids[j, 0:1, :] for j in range(4)], axis=1)
        scores = lax.dot_general(
            q_ref[...], keys, (((1,), (1,)), ((), ())), preferred_element_type=F32
        )
        own = segq[...]
        allowed = ids == jnp.concatenate([own] * 4, axis=1)
        if diagonal:
            place = lax.broadcasted_iota(jnp.int32, scores.shape, 1)
            token = lax.rem(lax.broadcasted_iota(jnp.int32, scores.shape, 0), ROWS) + y * ROWS
            allowed = allowed & (place <= token)
        scores = jnp.where(allowed, scores, NEG)
        before = top[...]
        now = jnp.maximum(before, jnp.max(scores, axis=1, keepdims=True))
        rate = math.log2(math.e) / math.sqrt(HD)
        keep = jnp.exp2((before - now) * rate)
        weights = jnp.exp2((scores - jnp.concatenate([now] * 4, axis=1)) * rate)
        part = (weights[:, 0:128] + weights[:, 128:256]) + (weights[:, 256:384] + weights[:, 384:512])
        top[...] = now
        den[...] = den[...] * keep + part
        acc[...] = acc[...] * keep + jnp.dot(weights.astype(BF16), values, preferred_element_type=F32)

    for i in (1, 3, 2):
        kv_z(i, True).start()
    plane_out(0)
    for i in (1, 3, 2):
        w_z(i, True).start()
    for i in range(1, 4):
        w_x(0, i, True).start()

    for r in (1, 3, 2):
        kv_z(r, False).wait_recv()
        plane_out(r)

    plane_in(0)
    kv_sib(0, 0, False).wait_recv()
    attend(h, x, True)

    def own_rows(dx, _):
        kv_sib(0, dx, False).wait_recv()

        @pl.when(dx <= x)
        def _():
            attend(h, x - dx, False)

        return 0

    lax.fori_loop(1, 4, own_rows, 0)

    for r in (1, 3, 2):
        plane_in(r)

        def rows(dx, _, r=r):
            kv_sib(r, dx, False).wait_recv()

            @pl.when(r <= h)
            def _():
                attend(h - r, mod4(x - dx), False)

            return 0

        lax.fori_loop(0, 4, rows, 0)
        w_z(r, False).wait_recv()
        for i in range(1, 4):
            w_x(r, i, True).start()

    out = acc[...] / jnp.sum(den[...], axis=1, keepdims=True)
    for head in range(4):
        for half in range(2):
            first = head * ROWS + half * 64
            asrc[half, :, head * HD : (head + 1) * HD] = out[first : first + 64].astype(BF16)
    for dy, dk in pairs:
        a_y(dy, dk, True).start()
    ar[k, y] = asrc[k]

    for r in (0, 1, 3, 2):
        for i in range(1, 4):
            w_x(r, i, False).wait_recv()
        w_sib(r, True).start()
    for r in (0, 1, 3, 2):
        w_sib(r, False).wait_recv()

    for dy, dk in pairs:
        a_y(dy, dk, False).wait_recv()

    def partial_for(dest):
        total = None
        for core in range(2):
            rows = ar[core].reshape(4 * 64, 4 * HD)
            columns = jnp.concatenate([wb[core, dest, j] for j in range(4)], axis=1)
            term = jnp.dot(rows, columns, preferred_element_type=F32)
            total = term if total is None else total + term
        return total

    for i in (2, 1, 3):
        pbuf[i] = partial_for(mod4(z + i)).astype(BF16)
        p_z(i, True).start()
    summed = partial_for(z)
    for i in (1, 3, 2):
        p_z(i, False).wait_recv()
        summed = summed + rb[mod4(z - i)].astype(F32)

    summed = summed.astype(BF16)
    for row in range(4):
        for core in range(2):
            for b in range(2):
                col = (core * 2 + b) * HD
                osrc[row, core, b] = summed[row * 64 : (row + 1) * 64, col : col + HD]
    for dy, dk in pairs:
        o_y(dy, dk, True).start()
    ob[k, y] = osrc[y, k]
    for dy, dk in pairs:
        o_y(dy, dk, False).wait_recv()
    for core in range(2):
        for row in range(4):
            for b in range(2):
                col = (b * 4 + row) * HD
                o_ref[core * 64 : (core + 1) * 64, col : col + HD] = ob[core, row, b]

    for i in range(1, 4):
        kv_z(i, True).wait_send()
        w_z(i, True).wait_send()
        p_z(i, True).wait_send()
    for r in range(4):

        def sent(d, _, r=r):
            kv_plane(r, d, True).wait_send()
            return 0

        lax.fori_loop(1, 16, sent, 0)

        def handed(dx, _, r=r):
            kv_sib(r, dx, True).wait_send()
            return 0

        lax.fori_loop(0, 4, handed, 0)
        for i in range(1, 4):
            w_x(r, i, True).wait_send()
        w_sib(r, True).wait_send()
    for dy, dk in pairs:
        a_y(dy, dk, True).wait_send()
        o_y(dy, dk, True).wait_send()


def body(queries, keys, values, segment_ids, out_weight):
    tpi = lax.axis_index("tp")
    head = tpi // 2
    mine = lax.dynamic_index_in_dim(jnp.where(tpi % 2 == 0, keys, values), head, 1, keepdims=False)
    q_rows = jnp.transpose(queries, (1, 0, 2)).reshape(4 * ROWS, HD)
    dma = pltpu.SemaphoreType.DMA
    return pl.pallas_call(
        kernel,
        out_shape=jax.ShapeDtypeStruct((ROWS, 1024), BF16),
        in_specs=[pl.BlockSpec(memory_space=pltpu.VMEM)] * 4,
        out_specs=pl.BlockSpec(memory_space=pltpu.VMEM),
        scratch_shapes=[
            pltpu.VMEM((2, 4, 16, BLK, HD), BF16),
            pltpu.VMEM((2, 4, 4, 512, HD), BF16),
            pltpu.VMEM((2, 64, 512), BF16),
            pltpu.VMEM((2, 4, 64, 512), BF16),
            pltpu.VMEM((4, 256, 512), BF16),
            pltpu.VMEM((4, 256, 512), BF16),
            pltpu.VMEM((4, 2, 2, 64, HD), BF16),
            pltpu.VMEM((2, 4, 2, 64, HD), BF16),
            pltpu.VMEM((512, HD), F32),
            pltpu.VMEM((512, HD), F32),
            pltpu.VMEM((512, HD), F32),
            pltpu.VMEM((512, HD), F32),
        ]
        + [dma((4,))] * 2
        + [dma((4, 16))] * 2
        + [dma((4, 4))] * 2
        + [dma((4,))] * 2
        + [dma((4, 4))] * 2
        + [dma((4,))] * 2
        + [dma((4, 2))] * 2
        + [dma((4,))] * 2
        + [dma((4, 2))] * 2,
        compiler_params=pltpu.CompilerParams(
            collective_id=0, has_side_effects=True, vmem_limit_bytes=48 << 20
        ),
        name="attention_projection",
    )(q_rows, mine, segment_ids.reshape(1, ROWS), out_weight)


def solution(mesh):
    in_specs = (
        P("ctx", "tp", None),
        P("ctx", None, None),
        P("ctx", None, None),
        P("ctx"),
        P("tp", "ctx"),
    )
    return jax.shard_map(body, mesh=mesh, in_specs=in_specs, out_specs=P("ctx", "tp"), check_vma=False)
```

time: 569 us -> 104 us (0.18)
  the two profiles are of different devices: /device:TPU:1 before, /device:TPU:33 now
where the time goes in v1:
time: 104 us
  Pallas kernels  100 us (96%)
  local copies, waits for them, and re-layouts  3.58 us (3%)
    pallas_call x1, Pallas kernels, body(): pl.pallas_call(kernel, out_shape=jax.ShapeDtypeStruct((ROWS, 1024), BF16)...  100 us
    unnamed x7, local copies, waits for them, and re-layouts  2.46 us

profile of v1, /device:TPU:33, one launch (start us, length us, event | category | flops | bytes accessed | tf_op | source)
XLA Modules:
  0.0 104.0 jit_solution(7337013100829205130)
XLA Ops:
  0.0 1.1 %constant_dynamic-slice_fusion = (bf16[128,1,128]{2,1,0:T(2,128)(2,1)S(1)}, bf16[128,1,128]{2,1,0:T(2,128)(2,1)S(1)}) fusion(bf16[128,4,128]{2,1,0:T(4,128)(2,1)} %param.6, s32[]{:T(128)S(6)} %select_n.27, bf16[128,4,128]{2,1,0:T(4,128)(2,1)} %param.7), kind=kLoop, calls=%fused_computation.2 | loop fusion | bytes 131076 | tf_op jit(solution)/shard_map/jit(dynamic_index_in_dim)/dynamic_slice | solution.py:299
  1.1 0.0 copy-start.2
  1.1 0.9 copy-done.2
  2.0 0.0 copy-start
  2.0 0.0 copy-start.1
  2.1 0.9 copy-done
  2.9 0.0 copy-done.1
  2.9 100.4 %attention_projection.1 = bf16[128,1024]{1,0:T(8,128)(2,1)S(1)} custom-call(bf16[512,128]{1,0:T(8,128)(2,1)S(1)} %bitcast.5, bf16[128,128]{1,0:T(8,128)(2,1)S(1)} %fusion.mine_ref, s32[1,128]{1,0:T(1,128)S(1)} %bitcast.6, bf16[512,128]{1,0:T(8,128)(2,1)S(1)} %copy-done), custom_call_target="tpu_custom_call" | custom-call | tf_op jit(solution)/shard_map/attention_projection/pallas_call | solution.py:302
  103.3 0.7 copy.17
  (2 shorter events, 0.0 us)
Async XLA Ops:
  1.1 0.9 copy-start.2
  2.0 0.9 copy-start
  2.0 0.9 copy-start.1

commit v2 on v1

v2 whole, which is shorter than its diff:
```python
import functools
import math

import jax
import jax.numpy as jnp
from jax import lax
from jax.experimental import pallas as pl
from jax.experimental.pallas import tpu as pltpu
from jax.sharding import PartitionSpec as P

HQ = 32
KVH = 4
HD = 128
ROWS = 128
SEG = 16
BLK = ROWS + SEG
NEG = -1e30
MESH = pl.DeviceIdType.MESH
BF16, F32 = jnp.bfloat16, jnp.float32


def mod4(value):
    return lax.rem(value + 8, 4)


def hadamard_signs():
    both = lax.broadcasted_iota(jnp.int32, (HD, HD), 0) & lax.broadcasted_iota(jnp.int32, (HD, HD), 1)
    both = both ^ (both >> 4)
    both = both ^ (both >> 2)
    both = both ^ (both >> 1)
    return (1 - 2 * (both & 1)).astype(F32).astype(BF16)


def kernel(
    q_ref, mine_ref, seg_ref, w_ref, o_ref,
    kv, wsrc, wb, asrc, ar, osrc, ob, segq, top, den, acc,
    kz_s, kz_r, ka_s, ka_r, kb_s, kb_r, ks_s, ks_r, wz_s, wz_r, wx_s, wx_r, ws_s, ws_r, az_s, az_r, ay_s, ay_r, o_s, o_r,
):
    ctx, tpi = lax.axis_index("ctx"), lax.axis_index("tp")
    h, x, y = lax.div(ctx, 16), lax.rem(lax.div(ctx, 4), 4), lax.rem(ctx, 4)
    z, k = lax.div(tpi, 2), lax.rem(tpi, 2)
    other = 1 - k
    first = x * other + y * k
    second = y * other + x * k

    def device(h_at, x_at, y_at, z_at, core):
        return (mod4(h_at) * 16 + mod4(x_at) * 4 + mod4(y_at), mod4(z_at) * 2 + core)

    def copy(src, dst, send, recv, target):
        return pltpu.make_async_remote_copy(
            src_ref=src, dst_ref=dst, send_sem=send, recv_sem=recv, device_id=target, device_id_type=MESH
        )

    sib = device(h, x, y, z, other)

    barrier = pltpu.get_barrier_semaphore()

    def greet(target):
        pl.semaphore_signal(barrier, inc=1, device_id=target, device_id_type=MESH)

    greet(sib)
    for i in range(1, 4):
        greet(device(h, x + i, y, z, k))
        greet(device(h, x, y + i, z, k))
        greet(device(h, x, y + i, z, other))
        greet(device(h, x, y, z + i, other))

    def greet_line(d, _):
        greet(device(h + lax.div(d, 4), x, y, z + lax.rem(d, 4), k))
        return 0

    lax.fori_loop(1, 16, greet_line, 0)

    kv[k, h, second, first, 0:ROWS, :] = mine_ref[...]
    seg_row = seg_ref[...].astype(F32)
    kv[k, h, second, first, ROWS:BLK, :] = jnp.broadcast_to(seg_row, (SEG, HD)).astype(BF16)
    rotated = jnp.dot(w_ref[...], hadamard_signs(), preferred_element_type=F32) * (1.0 / math.sqrt(HD))
    wsrc[...] = rotated.astype(BF16)
    seg_col = jnp.broadcast_to(seg_row, (ROWS, HD)).T
    for i in range(4):
        segq[i * ROWS : (i + 1) * ROWS, :] = seg_col
    top[...] = jnp.full_like(top, NEG)
    den[...] = jnp.zeros_like(den)
    acc[...] = jnp.zeros_like(acc)

    pl.semaphore_wait(barrier, 28)

    def kv_z(i, out):
        at = kv.at[k, h if out else mod4(h - i), second, first]
        return copy(at, at, kz_s.at[i], kz_r.at[i], device(h + i, x, y, z, k))

    def kv_first(r, i, out):
        at = kv.at[k, mod4(h - r), second, first if out else mod4(first - i)]
        return copy(at, at, ka_s.at[r, i], ka_r.at[r, i], device(h, x + i * other, y + i * k, z, k))

    def kv_second(r, i, out):
        at = kv.at[k, mod4(h - r), second if out else mod4(second - i)]
        return copy(at, at, kb_s.at[r, i], kb_r.at[r, i], device(h, x + i * k, y + i * other, z, k))

    def kv_sib(r, i, out):
        at = kv.at[k if out else other, mod4(h - r), mod4((second if out else first) - i)]
        return copy(at, at, ks_s.at[r, i], ks_r.at[r, i], sib)

    def w_out(i):
        return copy(wsrc, wb.at[k, z, x], wz_s.at[i], wz_r.at[z], device(h + i, x, y, h, k))

    def w_in(j):
        from_z = mod4(z + j)
        at = wb.at[k, from_z, x]
        return copy(at, at, wz_s.at[0], wz_r.at[from_z], device(z, x, y, from_z, k))

    def w_x(j, i, out):
        at = wb.at[k, mod4(z + j), x if out else mod4(x - i)]
        return copy(at, at, wx_s.at[j, i], wx_r.at[j, i], device(h, x + i, y, z, k))

    def w_sib(j, out):
        at = wb.at[k if out else other, mod4(z + j)]
        return copy(at, at, ws_s.at[j], ws_r.at[j], sib)

    def a_z(i, dk, out):
        core = lax.rem(k + dk, 2)
        dst = ar.at[z, k, y] if out else ar.at[mod4(z - i), core, y]
        return copy(asrc.at[core], dst, az_s.at[i, dk], az_r.at[i, dk], device(h, x, y, z + i, core))

    def a_y(i, dy, out):
        at = ar.at[mod4(z - i), :, y if out else mod4(y - dy)]
        return copy(at, at, ay_s.at[i, dy], ay_r.at[i, dy], device(h, x, y + dy, z, k))

    def o_y(dy, dk, out):
        core = lax.rem(k + dk, 2)
        dst = ob.at[k, y] if out else ob.at[core, mod4(y - dy)]
        return copy(osrc.at[mod4(y + dy), core], dst, o_s.at[dy, dk], o_r.at[dy, dk], device(h, x, y + dy, z, core))

    pairs = [(i, dk) for i in range(4) for dk in range(2) if i or dk]

    def first_out(r):
        for i in (2, 1, 3):
            kv_first(r, i, True).start()

    def second_out(r):
        for i in (1, 3, 2):
            kv_first(r, i, False).wait_recv()
        for i in (2, 1, 3):
            kv_second(r, i, True).start()
        kv_sib(r, 0, True).start()

    def sib_out(r):
        for i in (1, 3, 2):
            kv_second(r, i, False).wait_recv()
            kv_sib(r, i, True).start()

    def attend(hp, line, own_plane):
        keys = kv[0, hp, line, :, 0:ROWS, :].reshape(4 * ROWS, HD)
        values = kv[1, hp, :, pl.ds(line, 1), 0:ROWS, :].reshape(4 * ROWS, HD)
        ids = kv[0, hp, line, :, ROWS:BLK, :].astype(F32)
        ids = jnp.concatenate([ids[j, 0:1, :] for j in range(4)], axis=1)
        scores = lax.dot_general(
            q_ref[...], keys, (((1,), (1,)), ((), ())), preferred_element_type=F32
        )
        own = segq[...]
        allowed = ids == jnp.concatenate([own] * 4, axis=1)
        if own_plane:
            lane = lax.broadcasted_iota(jnp.int32, scores.shape, 1)
            place = lane + (lane >> 7) * (3 * ROWS) + line * ROWS
            token = (lax.broadcasted_iota(jnp.int32, scores.shape, 0) & (ROWS - 1)) + (x * 4 + y) * ROWS
            allowed = allowed & (place <= token)
        scores = jnp.where(allowed, scores, NEG)
        before = top[...]
        now = jnp.maximum(before, jnp.max(scores, axis=1, keepdims=True))
        rate = math.log2(math.e) / math.sqrt(HD)
        keep = jnp.exp2((before - now) * rate)
        weights = jnp.exp2((scores - jnp.concatenate([now] * 4, axis=1)) * rate)
        part = (weights[:, 0:128] + weights[:, 128:256]) + (weights[:, 256:384] + weights[:, 384:512])
        top[...] = now
        den[...] = den[...] * keep + part
        acc[...] = acc[...] * keep + jnp.dot(weights.astype(BF16), values, preferred_element_type=F32)

    def attend_plane(r):
        def line(i, _):
            kv_sib(r, i, False).wait_recv()
            return 0

        lax.fori_loop(0, 4, line, 0)

        def lines(i, _):
            attend(mod4(h - r), mod4(y - i), r == 0)
            return 0

        if r == 0:
            lax.fori_loop(0, 4, lines, 0)
        else:

            @pl.when(r <= h)
            def _():
                lax.fori_loop(0, 4, lines, 0)

    for i in (2, 1, 3):
        kv_z(i, True).start()
    first_out(0)
    second_out(0)
    for r in (1, 3):
        kv_z(r, False).wait_recv()
        first_out(r)
    for i in (2, 1, 3):
        w_out(i).start()

    @pl.when(h != z)
    def _():
        w_out(0).start()

    @pl.when(h == z)
    def _():
        wb[k, z, x] = wsrc[...]

    sib_out(0)
    for r in (1, 3):
        second_out(r)
    kv_z(2, False).wait_recv()
    first_out(2)
    sib_out(1)
    second_out(2)
    sib_out(3)

    attend_plane(0)
    attend_plane(1)
    attend_plane(3)
    sib_out(2)
    for j in range(4):
        if j == 0:

            @pl.when(h != z)
            def _():
                w_in(0).wait_recv()
        else:
            w_in(j).wait_recv()
        for i in range(1, 4):
            w_x(j, i, True).start()
    attend_plane(2)

    out = acc[...] / jnp.sum(den[...], axis=1, keepdims=True)
    for head in range(4):
        for half in range(2):
            start = head * ROWS + half * 64
            asrc[half, :, head * HD : (head + 1) * HD] = out[start : start + 64].astype(BF16)
    for i, dk in pairs:
        a_z(i, dk, True).start()
    ar[z, k, y] = asrc[k]
    for i in (0, 1, 3, 2):
        for dk in range(2):
            if i or dk:
                a_z(i, dk, False).wait_recv()
        for dy in (2, 1, 3):
            a_y(i, dy, True).start()

    for j in range(4):
        for i in range(1, 4):
            w_x(j, i, False).wait_recv()
        w_sib(j, True).start()
    for j in range(4):
        w_sib(j, False).wait_recv()

    total = None
    for i in (0, 1, 3, 2):
        for dy in (1, 3, 2):
            a_y(i, dy, False).wait_recv()
        from_z = mod4(z - i)
        for core in range(2):
            rows = ar[from_z, core].reshape(4 * 64, 4 * HD)
            columns = jnp.concatenate([wb[core, from_z, j] for j in range(4)], axis=1)
            term = jnp.dot(rows, columns, preferred_element_type=F32)
            total = term if total is None else total + term

    total = total.astype(BF16)
    for row in range(4):
        for core in range(2):
            for b in range(2):
                col = (core * 2 + b) * HD
                osrc[row, core, b] = total[row * 64 : (row + 1) * 64, col : col + HD]
    for dy, dk in pairs:
        o_y(dy, dk, True).start()
    ob[k, y] = osrc[y, k]
    for dy, dk in pairs:
        o_y(dy, dk, False).wait_recv()
    for core in range(2):
        for row in range(4):
            for b in range(2):
                col = (b * 4 + row) * HD
                o_ref[core * 64 : (core + 1) * 64, col : col + HD] = ob[core, row, b]

    for i in range(1, 4):
        kv_z(i, True).wait_send()
        w_out(i).wait_send()

    @pl.when(h != z)
    def _():
        w_out(0).wait_send()

    for r in range(4):
        for i in range(1, 4):
            kv_first(r, i, True).wait_send()
            kv_second(r, i, True).wait_send()
            w_x(r, i, True).wait_send()
            a_y(r, i, True).wait_send()
        for i in range(4):
            kv_sib(r, i, True).wait_send()
        w_sib(r, True).wait_send()
    for i, dk in pairs:
        a_z(i, dk, True).wait_send()
        o_y(i, dk, True).wait_send()


def body(queries, keys, values, segment_ids, out_weight):
    tpi = lax.axis_index("tp")
    head = tpi // 2
    mine = lax.dynamic_index_in_dim(jnp.where(tpi % 2 == 0, keys, values), head, 1, keepdims=False)
    q_rows = jnp.transpose(queries, (1, 0, 2)).reshape(4 * ROWS, HD)
    dma = pltpu.SemaphoreType.DMA
    return pl.pallas_call(
        kernel,
        out_shape=jax.ShapeDtypeStruct((ROWS, 1024), BF16),
        in_specs=[pl.BlockSpec(memory_space=pltpu.VMEM)] * 4,
        out_specs=pl.BlockSpec(memory_space=pltpu.VMEM),
        scratch_shapes=[
            pltpu.VMEM((2, 4, 4, 4, BLK, HD), BF16),
            pltpu.VMEM((512, HD), BF16),
            pltpu.VMEM((2, 4, 4, 512, HD), BF16),
            pltpu.VMEM((2, 64, 512), BF16),
            pltpu.VMEM((4, 2, 4, 64, 512), BF16),
            pltpu.VMEM((4, 2, 2, 64, HD), BF16),
            pltpu.VMEM((2, 4, 2, 64, HD), BF16),
            pltpu.VMEM((512, HD), F32),
            pltpu.VMEM((512, HD), F32),
            pltpu.VMEM((512, HD), F32),
            pltpu.VMEM((512, HD), F32),
        ]
        + [dma((4,))] * 2
        + [dma((4, 4))] * 6
        + [dma((4,))] * 2
        + [dma((4, 4))] * 2
        + [dma((4,))] * 2
        + [dma((4, 2))] * 2
        + [dma((4, 4))] * 2
        + [dma((4, 2))] * 2,
        compiler_params=pltpu.CompilerParams(
            collective_id=0, has_side_effects=True, vmem_limit_bytes=48 << 20
        ),
        name="attention_projection",
    )(q_rows, mine, segment_ids.reshape(1, ROWS), out_weight)


def solution(mesh):
    in_specs = (
        P("ctx", "tp", None),
        P("ctx", None, None),
        P("ctx", None, None),
        P("ctx"),
        P("tp", "ctx"),
    )
    return jax.shard_map(body, mesh=mesh, in_specs=in_specs, out_specs=P("ctx", "tp"), check_vma=False)
```

time: 104 us -> 97.2 us (0.935)
  the two profiles are of different devices: /device:TPU:33 before, /device:TPU:5 now
where the time goes in v2:
time: 97.2 us; the launch traced here: 97 us
  Pallas kernels  93.4 us (96%)
  local copies, waits for them, and re-layouts  3.58 us (4%)
    pallas_call x1, Pallas kernels, body(): pl.pallas_call(kernel, out_shape=jax.ShapeDtypeStruct((ROWS, 1024), BF16)...  93.4 us
    unnamed x7, local copies, waits for them, and re-layouts  2.46 us

profile of v2, /device:TPU:5, one launch (start us, length us, event | category | flops | bytes accessed | tf_op | source)
XLA Modules:
  0.0 97.0 jit_solution(13810388270277242712)
XLA Ops:
  0.0 1.1 %constant_dynamic-slice_fusion = (bf16[128,1,128]{2,1,0:T(2,128)(2,1)S(1)}, bf16[128,1,128]{2,1,0:T(2,128)(2,1)S(1)}) fusion(bf16[128,4,128]{2,1,0:T(4,128)(2,1)} %param.6, s32[]{:T(128)S(6)} %select_n.27, bf16[128,4,128]{2,1,0:T(4,128)(2,1)} %param.7), kind=kLoop, calls=%fused_computation.2 | loop fusion | bytes 131076 | tf_op jit(solution)/shard_map/jit(dynamic_index_in_dim)/dynamic_slice | solution.py:315
  1.1 0.0 copy-start.2
  1.1 0.9 copy-done.2
  2.0 0.0 copy-start
  2.0 0.0 copy-start.1
  2.1 0.9 copy-done
  2.9 0.0 copy-done.1
  2.9 93.4 %attention_projection.1 = bf16[128,1024]{1,0:T(8,128)(2,1)S(1)} custom-call(bf16[512,128]{1,0:T(8,128)(2,1)S(1)} %bitcast.5, bf16[128,128]{1,0:T(8,128)(2,1)S(1)} %fusion.mine_ref, s32[1,128]{1,0:T(1,128)S(1)} %bitcast.6, bf16[512,128]{1,0:T(8,128)(2,1)S(1)} %copy-done), custom_call_target="tpu_custom_call" | custom-call | tf_op jit(solution)/shard_map/attention_projection/pallas_call | solution.py:318
  96.3 0.7 copy.17
  (2 shorter events, 0.0 us)
Async XLA Ops:
  1.1 0.9 copy-start.2
  2.0 0.9 copy-start
  2.0 0.9 copy-start.1

commit v3 on v2

--- a/solution.py
+++ b/solution.py
@@ -101,21 +101,25 @@
         at = kv.at[k if out else other, mod4(h - r), mod4((second if out else first) - i)]
         return copy(at, at, ks_s.at[r, i], ks_r.at[r, i], sib)
 
-    def w_out(i):
-        return copy(wsrc, wb.at[k, z, x], wz_s.at[i], wz_r.at[z], device(h + i, x, y, h, k))
-
-    def w_in(j):
+    def depth(c):
+        return pl.ds(c * 256, 256)
+
+    def w_out(i, c):
+        dst = wb.at[k, z, x, depth(c)]
+        return copy(wsrc.at[depth(c)], dst, wz_s.at[c, i], wz_r.at[c, z], device(h + i, x, y, h, k))
+
+    def w_in(j, c):
         from_z = mod4(z + j)
-        at = wb.at[k, from_z, x]
-        return copy(at, at, wz_s.at[0], wz_r.at[from_z], device(z, x, y, from_z, k))
-
-    def w_x(j, i, out):
-        at = wb.at[k, mod4(z + j), x if out else mod4(x - i)]
-        return copy(at, at, wx_s.at[j, i], wx_r.at[j, i], device(h, x + i, y, z, k))
-
-    def w_sib(j, out):
-        at = wb.at[k if out else other, mod4(z + j)]
-        return copy(at, at, ws_s.at[j], ws_r.at[j], sib)
+        at = wb.at[k, from_z, x, depth(c)]
+        return copy(at, at, wz_s.at[c, 0], wz_r.at[c, from_z], device(z, x, y, from_z, k))
+
+    def w_x(j, i, c, out):
+        at = wb.at[k, mod4(z + j), x if out else mod4(x - i), depth(c)]
+        return copy(at, at, wx_s.at[c, j, i], wx_r.at[c, j, i], device(h, x + i, y, z, k))
+
+    def w_sib(j, c, out):
+        at = wb.at[k if out else other, mod4(z + j), :, depth(c)]
+        return copy(at, at, ws_s.at[c, j], ws_r.at[c, j], sib)
 
     def a_z(i, dk, out):
         core = lax.rem(k + dk, 2)
@@ -198,43 +202,42 @@
         kv_z(i, True).start()
     first_out(0)
     second_out(0)
-    for r in (1, 3):
+    for r in (1, 3, 2):
         kv_z(r, False).wait_recv()
         first_out(r)
-    for i in (2, 1, 3):
-        w_out(i).start()
-
-    @pl.when(h != z)
-    def _():
-        w_out(0).start()
+    for c in range(2):
+        for i in (2, 1, 3):
+            w_out(i, c).start()
+
+        @pl.when(h != z)
+        def _(c=c):
+            w_out(0, c).start()
 
     @pl.when(h == z)
     def _():
         wb[k, z, x] = wsrc[...]
 
+    for r in (1, 3, 2):
+        second_out(r)
+
+    def w_on(j, c):
+        if j == 0:
+
+            @pl.when(h != z)
+            def _():
+                w_in(0, c).wait_recv()
+        else:
+            w_in(j, c).wait_recv()
+        for i in (2, 1, 3):
+            w_x(j, i, c, True).start()
+
     sib_out(0)
-    for r in (1, 3):
-        second_out(r)
-    kv_z(2, False).wait_recv()
-    first_out(2)
+    attend_plane(0)
     sib_out(1)
-    second_out(2)
+    attend_plane(1)
     sib_out(3)
-
-    attend_plane(0)
-    attend_plane(1)
     attend_plane(3)
     sib_out(2)
-    for j in range(4):
-        if j == 0:
-
-            @pl.when(h != z)
-            def _():
-                w_in(0).wait_recv()
-        else:
-            w_in(j).wait_recv()
-        for i in range(1, 4):
-            w_x(j, i, True).start()
     attend_plane(2)
 
     out = acc[...] / jnp.sum(den[...], axis=1, keepdims=True)
@@ -245,19 +248,30 @@
     for i, dk in pairs:
         a_z(i, dk, True).start()
     ar[z, k, y] = asrc[k]
-    for i in (0, 1, 3, 2):
+    for j in range(4):
+        w_on(j, 0)
+
+    def a_on(i):
         for dk in range(2):
             if i or dk:
                 a_z(i, dk, False).wait_recv()
         for dy in (2, 1, 3):
             a_y(i, dy, True).start()
 
-    for j in range(4):
-        for i in range(1, 4):
-            w_x(j, i, False).wait_recv()
-        w_sib(j, True).start()
-    for j in range(4):
-        w_sib(j, False).wait_recv()
+    a_on(0)
+    for r in (1, 3, 2):
+        w_on({1:0,3:1,2:2}[r], 1)
+        a_on(r)
+    w_on(3, 1)
+
+    for c in range(2):
+        for j in range(4):
+            for i in range(1, 4):
+                w_x(j, i, c, False).wait_recv()
+            w_sib(j, c, True).start()
+    for c in range(2):
+        for j in range(4):
+            w_sib(j, c, False).wait_recv()
 
     total = None
     for i in (0, 1, 3, 2):
@@ -289,21 +303,25 @@
 
     for i in range(1, 4):
         kv_z(i, True).wait_send()
-        w_out(i).wait_send()
+        for c in range(2):
+            w_out(i, c).wait_send()
 
     @pl.when(h != z)
     def _():
-        w_out(0).wait_send()
+        for c in range(2):
+            w_out(0, c).wait_send()
 
     for r in range(4):
         for i in range(1, 4):
             kv_first(r, i, True).wait_send()
             kv_second(r, i, True).wait_send()
-            w_x(r, i, True).wait_send()
+            for c in range(2):
+                w_x(r, i, c, True).wait_send()
             a_y(r, i, True).wait_send()
         for i in range(4):
             kv_sib(r, i, True).wait_send()
-        w_sib(r, True).wait_send()
+        for c in range(2):
+            w_sib(r, c, True).wait_send()
     for i, dk in pairs:
         a_z(i, dk, True).wait_send()
         o_y(i, dk, True).wait_send()
@@ -335,9 +353,9 @@
         ]
         + [dma((4,))] * 2
         + [dma((4, 4))] * 6
-        + [dma((4,))] * 2
-        + [dma((4, 4))] * 2
-        + [dma((4,))] * 2
+        + [dma((2, 4))] * 2
+        + [dma((2, 4, 4))] * 2
+        + [dma((2, 4))] * 2
         + [dma((4, 2))] * 2
         + [dma((4, 4))] * 2
         + [dma((4, 2))] * 2,

time: 97.2 us -> 90.2 us (0.928)
  the two profiles are of different devices: /device:TPU:5 before, /device:TPU:1 now
where the time goes in v3:
time: 90.2 us; the launch traced here: 90 us
  Pallas kernels  86.4 us (96%)
  local copies, waits for them, and re-layouts  3.58 us (4%)
    pallas_call x1, Pallas kernels, body(): pl.pallas_call(kernel, out_shape=jax.ShapeDtypeStruct((ROWS, 1024), BF16)...  86.4 us
    unnamed x7, local copies, waits for them, and re-layouts  2.46 us

profile of v3, /device:TPU:1, one launch (start us, length us, event | category | flops | bytes accessed | tf_op | source)
XLA Modules:
  0.0 90.0 jit_solution(11545425784964809303)
XLA Ops:
  0.0 1.1 %constant_dynamic-slice_fusion = (bf16[128,1,128]{2,1,0:T(2,128)(2,1)S(1)}, bf16[128,1,128]{2,1,0:T(2,128)(2,1)S(1)}) fusion(bf16[128,4,128]{2,1,0:T(4,128)(2,1)} %param.6, s32[]{:T(128)S(6)} %select_n.27, bf16[128,4,128]{2,1,0:T(4,128)(2,1)} %param.7), kind=kLoop, calls=%fused_computation.2 | loop fusion | bytes 131076 | tf_op jit(solution)/shard_map/jit(dynamic_index_in_dim)/dynamic_slice | solution.py:333
  1.1 0.0 copy-start.2
  1.1 0.9 copy-done.2
  2.0 0.0 copy-start
  2.0 0.0 copy-start.1
  2.1 0.9 copy-done
  2.9 0.0 copy-done.1
  2.9 86.4 %attention_projection.1 = bf16[128,1024]{1,0:T(8,128)(2,1)S(1)} custom-call(bf16[512,128]{1,0:T(8,128)(2,1)S(1)} %bitcast.5, bf16[128,128]{1,0:T(8,128)(2,1)S(1)} %fusion.mine_ref, s32[1,128]{1,0:T(1,128)S(1)} %bitcast.6, bf16[512,128]{1,0:T(8,128)(2,1)S(1)} %copy-done), custom_call_target="tpu_custom_call" | custom-call | tf_op jit(solution)/shard_map/attention_projection/pallas_call | solution.py:336
  89.3 0.7 copy.17
  (2 shorter events, 0.0 us)
Async XLA Ops:
  1.1 0.9 %copy-start.2 = (bf16[128,4,128]{2,1,0:T(4,128)(2,1)S(1)}, bf16[128,4,128]{2,1,0:T(4,128)(2,1)}, u32[]{:S(2)}) copy-start(bf16[128,4,128]{2,1,0:T(4,128)(2,1)} %param.5) | copy-start | bytes 393220
  2.0 0.9 %copy-start = (bf16[512,128]{1,0:T(8,128)(2,1)S(1)}, bf16[512,128]{1,0:T(8,128)(2,1)}, u32[]{:S(2)}) copy-start(bf16[512,128]{1,0:T(8,128)(2,1)} %w_ref.1) | copy-start | bytes 393220
  2.0 0.9 copy-start.1

commit v4 on v3

--- a/solution.py
+++ b/solution.py
@@ -32,7 +32,8 @@
 
 
 def kernel(
-    q_ref, mine_ref, seg_ref, w_ref, o_ref,
+    q_in, k_in, v_in, seg_in, w_in_hbm, o_ref,
+    q_raw, kv_raw, seg_ref, w_ref, q_ref, in_sem,
     kv, wsrc, wb, asrc, ar, osrc, ob, segq, top, den, acc,
     kz_s, kz_r, ka_s, ka_r, kb_s, kb_r, ks_s, ks_r, wz_s, wz_r, wx_s, wx_r, ws_s, ws_r, az_s, az_r, ay_s, ay_r, o_s, o_r,
 ):
@@ -53,6 +54,21 @@
 
     sib = device(h, x, y, z, other)
 
+    def load(src, dst, i):
+        return pltpu.make_async_copy(src, dst, in_sem.at[i])
+
+    @pl.when(k == 0)
+    def _():
+        load(k_in, kv_raw, 0).start()
+
+    @pl.when(k == 1)
+    def _():
+        load(v_in, kv_raw, 0).start()
+
+    load(seg_in, seg_ref, 1).start()
+    load(w_in_hbm, w_ref, 2).start()
+    load(q_in, q_raw, 3).start()
+
     barrier = pltpu.get_barrier_semaphore()
 
     def greet(target):
@@ -71,11 +87,24 @@
 
     lax.fori_loop(1, 16, greet_line, 0)
 
-    kv[k, h, second, first, 0:ROWS, :] = mine_ref[...]
+    load(k_in, kv_raw, 0).wait()
+    by_head = kv_raw[...].astype(F32)
+    for head in range(KVH):
+
+        @pl.when(z == head)
+        def _(head=head):
+            kv[k, h, second, first, 0:ROWS, :] = by_head[:, head, :].astype(BF16)
+
+    load(seg_in, seg_ref, 1).wait()
     seg_row = seg_ref[...].astype(F32)
     kv[k, h, second, first, ROWS:BLK, :] = jnp.broadcast_to(seg_row, (SEG, HD)).astype(BF16)
+    load(w_in_hbm, w_ref, 2).wait()
     rotated = jnp.dot(w_ref[...], hadamard_signs(), preferred_element_type=F32) * (1.0 / math.sqrt(HD))
     wsrc[...] = rotated.astype(BF16)
+    load(q_in, q_raw, 3).wait()
+    by_head = q_raw[...].astype(F32)
+    for head in range(4):
+        q_ref[head * ROWS : (head + 1) * ROWS, :] = by_head[:, head, :].astype(BF16)
     seg_col = jnp.broadcast_to(seg_row, (ROWS, HD)).T
     for i in range(4):
         segq[i * ROWS : (i + 1) * ROWS, :] = seg_col
@@ -104,9 +133,12 @@
     def depth(c):
         return pl.ds(c * 256, 256)
 
-    def w_out(i, c):
+    def w_out(to, c):
         dst = wb.at[k, z, x, depth(c)]
-        return copy(wsrc.at[depth(c)], dst, wz_s.at[c, i], wz_r.at[c, z], device(h + i, x, y, h, k))
+        return copy(wsrc.at[depth(c)], dst, wz_s.at[c, to], wz_r.at[c, z], device(to, x, y, h, k))
+
+    def w_remote(to):
+        return (h != to) | (z != h)
 
     def w_in(j, c):
         from_z = mod4(z + j)
@@ -190,35 +222,47 @@
             attend(mod4(h - r), mod4(y - i), r == 0)
             return 0
 
-        if r == 0:
-            lax.fori_loop(0, 4, lines, 0)
-        else:
-
-            @pl.when(r <= h)
-            def _():
-                lax.fori_loop(0, 4, lines, 0)
+        lax.fori_loop(0, 4, lines, 0)
+
+    def w_start(to, also=True, parts=(0, 1)):
+        @pl.when(w_remote(to) & also)
+        def _():
+            for c in parts:
+                w_out(to, c).start()
+
+    def later(r, step):
+        @pl.when(r <= h)
+        def _():
+            step(r)
+
+    def passed_on(r):
+        kv_z(r, False).wait_recv()
+        first_out(r)
 
     for i in (2, 1, 3):
-        kv_z(i, True).start()
+
+        @pl.when(h + i <= 3)
+        def _(i=i):
+            kv_z(i, True).start()
+
     first_out(0)
     second_out(0)
-    for r in (1, 3, 2):
-        kv_z(r, False).wait_recv()
-        first_out(r)
-    for c in range(2):
-        for i in (2, 1, 3):
-            w_out(i, c).start()
-
-        @pl.when(h != z)
-        def _(c=c):
-            w_out(0, c).start()
+    for r in (1, 3):
+        later(r, passed_on)
+    w_start(0)
+    w_start(1, h > 0)
+    for to in range(1, 4):
+        w_start(to, h == 0, (0,))
+    later(2, passed_on)
 
     @pl.when(h == z)
     def _():
         wb[k, z, x] = wsrc[...]
 
     for r in (1, 3, 2):
-        second_out(r)
+        later(r, second_out)
+    w_start(2, h > 0)
+    w_start(3, h > 0)
 
     def w_on(j, c):
         if j == 0:
@@ -233,12 +277,9 @@
 
     sib_out(0)
     attend_plane(0)
-    sib_out(1)
-    attend_plane(1)
-    sib_out(3)
-    attend_plane(3)
-    sib_out(2)
-    attend_plane(2)
+    for r in (1, 3, 2):
+        later(r, sib_out)
+        later(r, attend_plane)
 
     out = acc[...] / jnp.sum(den[...], axis=1, keepdims=True)
     for head in range(4):
@@ -248,6 +289,8 @@
     for i, dk in pairs:
         a_z(i, dk, True).start()
     ar[z, k, y] = asrc[k]
+    for to in range(1, 4):
+        w_start(to, h == 0, (1,))
     for j in range(4):
         w_on(j, 0)
 
@@ -301,25 +344,32 @@
                 col = (b * 4 + row) * HD
                 o_ref[core * 64 : (core + 1) * 64, col : col + HD] = ob[core, row, b]
 
-    for i in range(1, 4):
-        kv_z(i, True).wait_send()
-        for c in range(2):
-            w_out(i, c).wait_send()
-
-    @pl.when(h != z)
-    def _():
-        for c in range(2):
-            w_out(0, c).wait_send()
-
-    for r in range(4):
+    def kv_left(r):
         for i in range(1, 4):
             kv_first(r, i, True).wait_send()
             kv_second(r, i, True).wait_send()
+        for i in range(4):
+            kv_sib(r, i, True).wait_send()
+
+    kv_left(0)
+    for r in range(1, 4):
+        later(r, kv_left)
+
+        @pl.when(h + r <= 3)
+        def _(r=r):
+            kv_z(r, True).wait_send()
+
+    for r in range(4):
+
+        @pl.when(w_remote(r))
+        def _(r=r):
+            for c in range(2):
+                w_out(r, c).wait_send()
+
+        for i in range(1, 4):
+            a_y(r, i, True).wait_send()
             for c in range(2):
                 w_x(r, i, c, True).wait_send()
-            a_y(r, i, True).wait_send()
-        for i in range(4):
-            kv_sib(r, i, True).wait_send()
         for c in range(2):
             w_sib(r, c, True).wait_send()
     for i, dk in pairs:
@@ -328,17 +378,19 @@
 
 
 def body(queries, keys, values, segment_ids, out_weight):
-    tpi = lax.axis_index("tp")
-    head = tpi // 2
-    mine = lax.dynamic_index_in_dim(jnp.where(tpi % 2 == 0, keys, values), head, 1, keepdims=False)
-    q_rows = jnp.transpose(queries, (1, 0, 2)).reshape(4 * ROWS, HD)
     dma = pltpu.SemaphoreType.DMA
     return pl.pallas_call(
         kernel,
         out_shape=jax.ShapeDtypeStruct((ROWS, 1024), BF16),
-        in_specs=[pl.BlockSpec(memory_space=pltpu.VMEM)] * 4,
+        in_specs=[pl.BlockSpec(memory_space=pl.ANY)] * 5,
         out_specs=pl.BlockSpec(memory_space=pltpu.VMEM),
         scratch_shapes=[
+            pltpu.VMEM((ROWS, 4, HD), BF16),
+            pltpu.VMEM((ROWS, KVH, HD), BF16),
+            pltpu.VMEM((1, ROWS), jnp.int32),
+            pltpu.VMEM((512, HD), BF16),
+            pltpu.VMEM((512, HD), BF16),
+            dma((4,)),
             pltpu.VMEM((2, 4, 4, 4, BLK, HD), BF16),
             pltpu.VMEM((512, HD), BF16),
             pltpu.VMEM((2, 4, 4, 512, HD), BF16),
@@ -360,10 +412,10 @@
         + [dma((4, 4))] * 2
         + [dma((4, 2))] * 2,
         compiler_params=pltpu.CompilerParams(
-            collective_id=0, has_side_effects=True, vmem_limit_bytes=48 << 20
+            collective_id=0, has_side_effects=True, vmem_limit_bytes=60 << 20
         ),
         name="attention_projection",
-    )(q_rows, mine, segment_ids.reshape(1, ROWS), out_weight)
+    )(queries, keys, values, segment_ids.reshape(1, ROWS), out_weight)
 
 
 def solution(mesh):

time: 90.2 us -> 83.8 us (0.929)
  Pallas kernels: 86.4 us -> 81.9 us
  local copies, waits for them, and re-layouts: 3.58 us -> 1.67 us
    pallas_call x1, Pallas kernels: 86.4 us -> 81.9 us  [body(): pl.pallas_call(kernel, out_shape=jax.ShapeDtypeStruct((ROWS, 1024), BF16)...]
    dynamic_slice x1 -> x0, local copies, waits for them, and re-layouts: 1.11 us -> none  [body(): lax.dynamic_index_in_dim(jnp.where(tpi % 2 == 0, keys, values), head, 1,...]
    unnamed x7 -> x1, local copies, waits for them, and re-layouts: 2.46 us -> 1.67 us
where the time goes in v4:
time: 83.8 us; the launch traced here: 83.6 us
  Pallas kernels  81.9 us (98%)
  local copies, waits for them, and re-layouts  1.67 us (2%)
    pallas_call x1, Pallas kernels, body(): pl.pallas_call(kernel, out_shape=jax.ShapeDtypeStruct((ROWS, 1024), BF16)...  81.9 us

profile of v4, /device:TPU:1, one launch (start us, length us, event | category | flops | bytes accessed | tf_op | source)
XLA Modules:
  0.0 83.6 jit_solution(17097821907952400182)
XLA Ops:
  0.0 81.9 %attention_projection.1 = bf16[128,1024]{1,0:T(8,128)(2,1)} custom-call(bf16[128,4,128]{2,1,0:T(4,128)(2,1)} %q_in.1, bf16[128,4,128]{2,1,0:T(4,128)(2,1)} %k_in.1, bf16[128,4,128]{2,1,0:T(4,128)(2,1)} %v_in.1, s32[1,128]{1,0:T(1,128)} %bitcast.1, bf16[512,128]{1,0:T(8,128)(2,1)} %w_in_hbm.1), custom_call_target="tpu_custom_call" | custom-call | tf_op jit(solution)/shard_map/attention_projection/pallas_call | solution.py:382
  81.9 1.7 %copy.7 = bf16[128,1024]{1,0:T(8,128)(2,1)} copy(bf16[128,1024]{1,0:T(8,128)(2,1)} %attention_projection.1) | data formatting | bytes 524288

commit v5 on v4

--- a/solution.py
+++ b/solution.py
@@ -98,20 +98,6 @@
     load(seg_in, seg_ref, 1).wait()
     seg_row = seg_ref[...].astype(F32)
     kv[k, h, second, first, ROWS:BLK, :] = jnp.broadcast_to(seg_row, (SEG, HD)).astype(BF16)
-    load(w_in_hbm, w_ref, 2).wait()
-    rotated = jnp.dot(w_ref[...], hadamard_signs(), preferred_element_type=F32) * (1.0 / math.sqrt(HD))
-    wsrc[...] = rotated.astype(BF16)
-    load(q_in, q_raw, 3).wait()
-    by_head = q_raw[...].astype(F32)
-    for head in range(4):
-        q_ref[head * ROWS : (head + 1) * ROWS, :] = by_head[:, head, :].astype(BF16)
-    seg_col = jnp.broadcast_to(seg_row, (ROWS, HD)).T
-    for i in range(4):
-        segq[i * ROWS : (i + 1) * ROWS, :] = seg_col
-    top[...] = jnp.full_like(top, NEG)
-    den[...] = jnp.zeros_like(den)
-    acc[...] = jnp.zeros_like(acc)
-
     pl.semaphore_wait(barrier, 28)
 
     def kv_z(i, out):
@@ -246,6 +232,21 @@
             kv_z(i, True).start()
 
     first_out(0)
+
+    load(w_in_hbm, w_ref, 2).wait()
+    rotated = jnp.dot(w_ref[...], hadamard_signs(), preferred_element_type=F32) * (1.0 / math.sqrt(HD))
+    wsrc[...] = rotated.astype(BF16)
+    load(q_in, q_raw, 3).wait()
+    by_head = q_raw[...].astype(F32)
+    for head in range(4):
+        q_ref[head * ROWS : (head + 1) * ROWS, :] = by_head[:, head, :].astype(BF16)
+    seg_col = jnp.broadcast_to(seg_row, (ROWS, HD)).T
+    for i in range(4):
+        segq[i * ROWS : (i + 1) * ROWS, :] = seg_col
+    top[...] = jnp.full_like(top, NEG)
+    den[...] = jnp.zeros_like(den)
+    acc[...] = jnp.zeros_like(acc)
+
     second_out(0)
     for r in (1, 3):
         later(r, passed_on)
@@ -291,9 +292,6 @@
     ar[z, k, y] = asrc[k]
     for to in range(1, 4):
         w_start(to, h == 0, (1,))
-    for j in range(4):
-        w_on(j, 0)
-
     def a_on(i):
         for dk in range(2):
             if i or dk:
@@ -302,8 +300,10 @@
             a_y(i, dy, True).start()
 
     a_on(0)
-    for r in (1, 3, 2):
-        w_on({1:0,3:1,2:2}[r], 1)
+    for j in range(4):
+        w_on(j, 0)
+    for j, r in enumerate((1, 3, 2)):
+        w_on(j, 1)
         a_on(r)
     w_on(3, 1)
 

time: 83.8 us -> 83.8 us (level)
  no operation moved by 1% of the time
where the time goes in v5:
time: 83.8 us; the launch traced here: 83.6 us
  Pallas kernels  81.9 us (98%)
  local copies, waits for them, and re-layouts  1.67 us (2%)
    pallas_call x1, Pallas kernels, body(): pl.pallas_call(kernel, out_shape=jax.ShapeDtypeStruct((ROWS, 1024), BF16)...  81.9 us

profile of v5, /device:TPU:1, one launch (start us, length us, event | category | flops | bytes accessed | tf_op | source)
XLA Modules:
  0.0 83.6 jit_solution(2301672449368467803)
XLA Ops:
  0.0 81.9 %attention_projection.1 = bf16[128,1024]{1,0:T(8,128)(2,1)} custom-call(bf16[128,4,128]{2,1,0:T(4,128)(2,1)} %q_in.1, bf16[128,4,128]{2,1,0:T(4,128)(2,1)} %k_in.1, bf16[128,4,128]{2,1,0:T(4,128)(2,1)} %v_in.1, s32[1,128]{1,0:T(1,128)} %bitcast.1, bf16[512,128]{1,0:T(8,128)(2,1)} %w_in_hbm.1), custom_call_target="tpu_custom_call" | custom-call | tf_op jit(solution)/shard_map/attention_projection/pallas_call | solution.py:382
  81.9 1.7 %copy.7 = bf16[128,1024]{1,0:T(8,128)(2,1)} copy(bf16[128,1024]{1,0:T(8,128)(2,1)} %attention_projection.1) | data formatting | bytes 524288

commit v6 on v5

--- a/solution.py
+++ b/solution.py
@@ -296,7 +296,7 @@
         for dk in range(2):
             if i or dk:
                 a_z(i, dk, False).wait_recv()
-        for dy in (2, 1, 3):
+        for dy in (1, 3, 2):
             a_y(i, dy, True).start()
 
     a_on(0)

time: 83.8 us -> 83.7 us (level)
  no operation moved by 1% of the time
where the time goes in v6:
time: 83.7 us; the launch traced here: 83.3 us
  Pallas kernels  81.7 us (98%)
  local copies, waits for them, and re-layouts  1.67 us (2%)
    pallas_call x1, Pallas kernels, body(): pl.pallas_call(kernel, out_shape=jax.ShapeDtypeStruct((ROWS, 1024), BF16)...  81.7 us

profile of v6, /device:TPU:1, one launch (start us, length us, event | category | flops | bytes accessed | tf_op | source)
XLA Modules:
  0.0 83.3 jit_solution(11590214447936327186)
XLA Ops:
  0.0 81.7 %attention_projection.1 = bf16[128,1024]{1,0:T(8,128)(2,1)} custom-call(bf16[128,4,128]{2,1,0:T(4,128)(2,1)} %q_in.1, bf16[128,4,128]{2,1,0:T(4,128)(2,1)} %k_in.1, bf16[128,4,128]{2,1,0:T(4,128)(2,1)} %v_in.1, s32[1,128]{1,0:T(1,128)} %bitcast.1, bf16[512,128]{1,0:T(8,128)(2,1)} %w_in_hbm.1), custom_call_target="tpu_custom_call" | custom-call | tf_op jit(solution)/shard_map/attention_projection/pallas_call | solution.py:382
  81.7 1.7 %copy.7 = bf16[128,1024]{1,0:T(8,128)(2,1)} copy(bf16[128,1024]{1,0:T(8,128)(2,1)} %attention_projection.1) | data formatting | bytes 524288
